TPU v7x, 32 devices: a whole 2x2x4 slice. The times are simulated.
32 devices in a mesh: dp: 8 (over z, x), tensor: 4 (over y, core).
Axes of the slice: x: 2, y: 2, z: 4, core: 2. Of those that a mesh axis runs over, the one named last changes fastest.
Arguments:
- layer_input: float32 [8, 1024, 768], P('dp', 'tensor'), may hold values from -40 to 40
- out_cotangent: float32 [8, 1024, 768], P('dp', 'tensor'), may hold values from -6 to 6
- mix_gain: bfloat16 [768], P('dp'), may hold values from 0.099609375 to 1.8984375
- mix_shift: bfloat16 [768], P('dp'), may hold values from -4 to 4
- query_weight: bfloat16 [768, 768], P('dp', 'tensor'), may hold values from -2 to 2
- query_bias: bfloat16 [64, 12], P('dp', 'tensor'), may hold values from -3 to 3
- key_weight: bfloat16 [768, 768], P('dp', 'tensor'), may hold values from -2 to 2
- value_weight: bfloat16 [768, 768], P('dp', 'tensor'), may hold values from -0.21875 to 0.21875
- value_bias: bfloat16 [64, 12], P('dp', 'tensor'), may hold values from -0.59765625 to 0.59765625
- output_weight: bfloat16 [768, 768], P('dp', 'tensor'), may hold values from -1.75 to 1.75
- output_bias: bfloat16 [768], P('dp'), may hold values from -4 to 4
- feed_gain: bfloat16 [768], P('dp'), may hold values from 0.099609375 to 1.8984375
- feed_shift: bfloat16 [768], P('dp'), may hold values from -4 to 4
- inner_weight: bfloat16 [768, 3072], P('dp', 'tensor'), may hold values from -0.21875 to 0.21875
- inner_bias: bfloat16 [64, 48], P('dp', 'tensor'), may hold values from -3 to 3
- outer_weight: bfloat16 [768, 3072], P('dp', 'tensor'), may hold values from -0.3125 to 0.3125
- outer_bias: bfloat16 [768], P('dp'), may hold values from -4 to 4
Outputs:
- layer_output: float32 [8, 1024, 768], P('dp', 'tensor')
- input_grad: float32 [8, 1024, 768], P('dp', 'tensor')
- mix_gain_grad: float32 [768], P(('dp', 'tensor'))
- mix_shift_grad: float32 [768], P(('dp', 'tensor'))
- query_weight_grad: float32 [768, 768], P('dp', 'tensor')
- query_bias_grad: float32 [64, 12], P('dp', 'tensor')
- key_weight_grad: float32 [768, 768], P('dp', 'tensor')
- value_weight_grad: float32 [768, 768], P('dp', 'tensor')
- value_bias_grad: float32 [64, 12], P('dp', 'tensor')
- output_weight_grad: float32 [768, 768], P('dp', 'tensor')
- output_bias_grad: float32 [768], P(('dp', 'tensor'))
- feed_gain_grad: float32 [768], P(('dp', 'tensor'))
- feed_shift_grad: float32 [768], P(('dp', 'tensor'))
- inner_weight_grad: float32 [768, 3072], P('dp', 'tensor')
- inner_bias_grad: float32 [64, 48], P('dp', 'tensor')
- outer_weight_grad: float32 [768, 3072], P('dp', 'tensor')
- outer_bias_grad: float32 [768], P(('dp', 'tensor'))
All inputs are finite; a program needn't handle non-finite values.
Results may differ from a plain program's by a relative error of at most 0.02.
Values may be sent and summed in bfloat16 or wider, within the bound.
A program may use at most 128 MiB of HBM per device.

v0:
```python
import math
import jax
import jax.numpy as jnp
from jax import lax
from jax.sharding import PartitionSpec as P

HD = 64
EPS = 1e-05
ROOT_HALF = 0.7071067811865476
DENSITY_NORM = 0.3989422804014327


def layer_norm(block, gain, shift):
    row_mean = jnp.mean(block, axis=-1, keepdims=True)
    centred = block - row_mean
    rstd = lax.rsqrt(jnp.mean(centred * centred, axis=-1, keepdims=True) + EPS)
    normed = centred * rstd
    lowered = (normed * gain.astype(jnp.float32) + shift.astype(jnp.float32)).astype(jnp.bfloat16)
    return (normed, rstd, lowered)


def norm_backward(gradient, normed, rstd, gain):
    scaled = gradient * gain.astype(jnp.float32)
    first = jnp.mean(scaled, axis=-1, keepdims=True)
    second = jnp.mean(scaled * normed, axis=-1, keepdims=True)
    return (scaled - first - normed * second) * rstd


def gelu_value(preact):
    return 0.5 * preact * (1.0 + lax.erf(preact * ROOT_HALF))


def gelu_slope(preact):
    return 0.5 * (1.0 + lax.erf(preact * ROOT_HALF)) + preact * DENSITY_NORM * jnp.exp(
        -0.5 * preact * preact
    )


def matmul(left, right):
    return jnp.dot(left, right, preferred_element_type=jnp.float32)


def token_product(left, right):
    return lax.dot_general(
        left, right, (((0,), (0,)), ((), ())), preferred_element_type=jnp.float32
    )


def split_heads(block):
    return block.reshape(block.shape[0], block.shape[1] // HD, HD)


def attend(operands):
    queries, key_rows, values = operands
    score_scale = 1.0 / math.sqrt(HD)
    scores = (
        jnp.einsum(
            "qhd,khd->hqk",
            split_heads(queries),
            split_heads(key_rows),
            preferred_element_type=jnp.float32,
        )
        * score_scale
    )
    row_max = jnp.max(scores, axis=-1, keepdims=True)
    log_total = row_max + jnp.log(jnp.sum(jnp.exp(scores - row_max), axis=-1, keepdims=True))
    prob_low = jnp.exp(scores - log_total).astype(jnp.bfloat16)
    context = jnp.einsum(
        "hqk,khd->qhd", prob_low, split_heads(values), preferred_element_type=jnp.float32
    )
    return (context.reshape(queries.shape).astype(jnp.bfloat16), log_total)


def attend_back(operands):
    queries, key_rows, values, context_grad, log_total = operands
    score_scale = 1.0 / math.sqrt(HD)
    query_heads = split_heads(queries)
    key_heads = split_heads(key_rows)
    grad_heads = split_heads(context_grad)
    scores = (
        jnp.einsum("qhd,khd->hqk", query_heads, key_heads, preferred_element_type=jnp.float32)
        * score_scale
    )
    prob_full = jnp.exp(scores - log_total)
    prob_low = prob_full.astype(jnp.bfloat16)
    value_grad = jnp.einsum(
        "hqk,qhd->khd", prob_low, grad_heads, preferred_element_type=jnp.float32
    )
    prob_grad = jnp.einsum(
        "qhd,khd->hqk", grad_heads, split_heads(values), preferred_element_type=jnp.float32
    )
    row_dot = jnp.sum(prob_full * prob_grad, axis=-1, keepdims=True)
    score_grad = (prob_full * (prob_grad - row_dot) * score_scale).astype(jnp.bfloat16)
    query_grad = jnp.einsum(
        "hqk,khd->qhd", score_grad, key_heads, preferred_element_type=jnp.float32
    )
    key_low = jnp.einsum(
        "hqk,qhd->khd", score_grad, query_heads, preferred_element_type=jnp.float32
    ).astype(jnp.bfloat16)
    return (
        query_grad.reshape(queries.shape),
        key_low.reshape(queries.shape),
        value_grad.reshape(queries.shape),
    )


def on_device(
    layer_input,
    out_cotangent,
    mix_gain,
    mix_shift,
    query_weight,
    query_bias,
    key_weight,
    value_weight,
    value_bias,
    output_weight,
    output_bias,
    feed_gain,
    feed_shift,
    inner_weight,
    inner_bias,
    outer_weight,
    outer_bias,
):
    (
        gain_first,
        shift_first,
        query_full,
        bias_query,
        key_full,
        value_full,
        bias_value,
        output_full,
        bias_output,
        gain_second,
        shift_second,
        inner_full,
        bias_inner,
        outer_full,
        bias_outer,
    ) = (
        lax.all_gather(mix_gain, "dp", axis=0, tiled=True),
        lax.all_gather(mix_shift, "dp", axis=0, tiled=True),
        lax.all_gather(query_weight, "dp", axis=0, tiled=True),
        lax.all_gather(query_bias, "dp", axis=0, tiled=True),
        lax.all_gather(key_weight, "dp", axis=0, tiled=True),
        lax.all_gather(value_weight, "dp", axis=0, tiled=True),
        lax.all_gather(value_bias, "dp", axis=0, tiled=True),
        lax.all_gather(output_weight, "dp", axis=0, tiled=True),
        lax.all_gather(output_bias, "dp", axis=0, tiled=True),
        lax.all_gather(feed_gain, "dp", axis=0, tiled=True),
        lax.all_gather(feed_shift, "dp", axis=0, tiled=True),
        lax.all_gather(inner_weight, "dp", axis=0, tiled=True),
        lax.all_gather(inner_bias, "dp", axis=0, tiled=True),
        lax.all_gather(outer_weight, "dp", axis=0, tiled=True),
        lax.all_gather(outer_bias, "dp", axis=0, tiled=True),
    )
    clip_count = layer_input.shape[0]
    feature_count = layer_input.shape[2]
    normed_one, rstd_one, lowered_one = layer_norm(layer_input, gain_first, shift_first)
    gathered_one = lax.all_gather(lowered_one, "tensor", axis=1, tiled=True)
    frames = gathered_one.shape[1]
    flat_one = gathered_one.reshape(clip_count * frames, feature_count)
    vector_query = bias_query.astype(jnp.float32).T.reshape(-1)
    vector_value = bias_value.astype(jnp.float32).T.reshape(-1)
    vector_inner = bias_inner.astype(jnp.float32).T.reshape(-1)
    width = query_full.shape[1]
    queries = (matmul(flat_one, query_full) + vector_query).astype(jnp.bfloat16)
    key_rows = matmul(flat_one, key_full).astype(jnp.bfloat16)
    values = (matmul(flat_one, value_full) + vector_value).astype(jnp.bfloat16)
    clip_queries = queries.reshape(clip_count, frames, width)
    clip_keys = key_rows.reshape(clip_count, frames, width)
    clip_values = values.reshape(clip_count, frames, width)
    context, log_total = lax.map(attend, (clip_queries, clip_keys, clip_values))
    flat_context = context.reshape(clip_count * frames, width)
    attn_partial = matmul(flat_context, output_full.T).reshape(clip_count, frames, feature_count)
    attn_share = lax.psum_scatter(
        attn_partial.astype(jnp.bfloat16), "tensor", scatter_dimension=1, tiled=True
    ).astype(jnp.float32)
    mixed = layer_input + attn_share + bias_output.astype(jnp.float32)
    normed_two, rstd_two, lowered_two = layer_norm(mixed, gain_second, shift_second)
    gathered_two = lax.all_gather(lowered_two, "tensor", axis=1, tiled=True)
    flat_two = gathered_two.reshape(clip_count * frames, feature_count)
    preact = matmul(flat_two, inner_full) + vector_inner
    hidden = gelu_value(preact).astype(jnp.bfloat16)
    feed_partial = matmul(hidden, outer_full.T).reshape(clip_count, frames, feature_count)
    feed_share = lax.psum_scatter(
        feed_partial.astype(jnp.bfloat16), "tensor", scatter_dimension=1, tiled=True
    ).astype(jnp.float32)
    layer_output = mixed + feed_share + bias_outer.astype(jnp.float32)
    cot_low = out_cotangent.astype(jnp.bfloat16)
    cot_all = lax.all_gather(cot_low, "tensor", axis=1, tiled=True).reshape(
        clip_count * frames, feature_count
    )
    preact_grad = matmul(cot_all, outer_full) * gelu_slope(preact)
    preact_low = preact_grad.astype(jnp.bfloat16)
    outer_grad = token_product(cot_all, hidden)
    inner_grad = token_product(flat_two, preact_low)
    inner_bias_part = jnp.sum(preact_grad, axis=0).reshape(-1, HD).T
    norm_two_part = matmul(preact_low, inner_full.T).reshape(clip_count, frames, feature_count)
    norm_two_grad = lax.psum_scatter(
        norm_two_part.astype(jnp.bfloat16), "tensor", scatter_dimension=1, tiled=True
    ).astype(jnp.float32)
    feed_gain_part = jnp.sum(norm_two_grad * normed_two, axis=(0, 1))
    feed_shift_part = jnp.sum(norm_two_grad, axis=(0, 1))
    mixed_grad = out_cotangent + norm_backward(norm_two_grad, normed_two, rstd_two, gain_second)
    outer_bias_part = jnp.sum(out_cotangent, axis=(0, 1))
    output_bias_part = jnp.sum(mixed_grad, axis=(0, 1))
    mixed_low = mixed_grad.astype(jnp.bfloat16)
    mixed_all = lax.all_gather(mixed_low, "tensor", axis=1, tiled=True).reshape(
        clip_count * frames, feature_count
    )
    output_grad = token_product(mixed_all, flat_context)
    context_grad = (
        matmul(mixed_all, output_full).astype(jnp.bfloat16).reshape(clip_count, frames, width)
    )
    query_grad, key_low, value_grad = lax.map(
        attend_back, (clip_queries, clip_keys, clip_values, context_grad, log_total)
    )
    query_grad = query_grad.reshape(clip_count * frames, width)
    key_low = key_low.reshape(clip_count * frames, width)
    value_grad = value_grad.reshape(clip_count * frames, width)
    query_low = query_grad.astype(jnp.bfloat16)
    value_low = value_grad.astype(jnp.bfloat16)
    query_grad_part = token_product(flat_one, query_low)
    key_grad_part = token_product(flat_one, key_low)
    value_grad_part = token_product(flat_one, value_low)
    query_bias_part = jnp.sum(query_grad, axis=0).reshape(-1, HD).T
    value_bias_part = jnp.sum(value_grad, axis=0).reshape(-1, HD).T
    norm_one_part = (
        matmul(query_low, query_full.T)
        + matmul(key_low, key_full.T)
        + matmul(value_low, value_full.T)
    )
    norm_one_grad = lax.psum_scatter(
        norm_one_part.reshape(clip_count, frames, feature_count).astype(jnp.bfloat16),
        "tensor",
        scatter_dimension=1,
        tiled=True,
    ).astype(jnp.float32)
    mix_gain_part = jnp.sum(norm_one_grad * normed_one, axis=(0, 1))
    mix_shift_part = jnp.sum(norm_one_grad, axis=(0, 1))
    input_grad = mixed_grad + norm_backward(norm_one_grad, normed_one, rstd_one, gain_first)
    (
        query_weight_grad,
        query_bias_grad,
        key_weight_grad,
        value_weight_grad,
        value_bias_grad,
        output_weight_grad,
        inner_weight_grad,
        inner_bias_grad,
        outer_weight_grad,
    ) = (
        lax.psum_scatter(query_grad_part, "dp", scatter_dimension=0, tiled=True),
        lax.psum_scatter(query_bias_part, "dp", scatter_dimension=0, tiled=True),
        lax.psum_scatter(key_grad_part, "dp", scatter_dimension=0, tiled=True),
        lax.psum_scatter(value_grad_part, "dp", scatter_dimension=0, tiled=True),
        lax.psum_scatter(value_bias_part, "dp", scatter_dimension=0, tiled=True),
        lax.psum_scatter(output_grad, "dp", scatter_dimension=0, tiled=True),
        lax.psum_scatter(inner_grad, "dp", scatter_dimension=0, tiled=True),
        lax.psum_scatter(inner_bias_part, "dp", scatter_dimension=0, tiled=True),
        lax.psum_scatter(outer_grad, "dp", scatter_dimension=0, tiled=True),
    )
    (
        mix_gain_grad,
        mix_shift_grad,
        output_bias_grad,
        feed_gain_grad,
        feed_shift_grad,
        outer_bias_grad,
    ) = (
        lax.psum_scatter(mix_gain_part, ("dp", "tensor"), scatter_dimension=0, tiled=True),
        lax.psum_scatter(mix_shift_part, ("dp", "tensor"), scatter_dimension=0, tiled=True),
        lax.psum_scatter(output_bias_part, ("dp", "tensor"), scatter_dimension=0, tiled=True),
        lax.psum_scatter(feed_gain_part, ("dp", "tensor"), scatter_dimension=0, tiled=True),
        lax.psum_scatter(feed_shift_part, ("dp", "tensor"), scatter_dimension=0, tiled=True),
        lax.psum_scatter(outer_bias_part, ("dp", "tensor"), scatter_dimension=0, tiled=True),
    )
    return (
        layer_output,
        input_grad,
        mix_gain_grad,
        mix_shift_grad,
        query_weight_grad,
        query_bias_grad,
        key_weight_grad,
        value_weight_grad,
        value_bias_grad,
        output_weight_grad,
        output_bias_grad,
        feed_gain_grad,
        feed_shift_grad,
        inner_weight_grad,
        inner_bias_grad,
        outer_weight_grad,
        outer_bias_grad,
    )


def solution(mesh):
    placed = (
        P("dp", "tensor", None),
        P("dp", "tensor", None),
        P("dp"),
        P("dp"),
        P("dp", "tensor"),
        P("dp", "tensor"),
        P("dp", "tensor"),
        P("dp", "tensor"),
        P("dp", "tensor"),
        P("dp", "tensor"),
        P("dp"),
        P("dp"),
        P("dp"),
        P("dp", "tensor"),
        P("dp", "tensor"),
        P("dp", "tensor"),
        P("dp"),
    )
    return jax.shard_map(
        on_device,
        mesh=mesh,
        in_specs=placed,
        out_specs=(
            P("dp", "tensor", None),
            P("dp", "tensor", None),
            P(("dp", "tensor")),
            P(("dp", "tensor")),
            P("dp", "tensor"),
            P("dp", "tensor"),
            P("dp", "tensor"),
            P("dp", "tensor"),
            P("dp", "tensor"),
            P("dp", "tensor"),
            P(("dp", "tensor")),
            P(("dp", "tensor")),
            P(("dp", "tensor")),
            P("dp", "tensor"),
            P("dp", "tensor"),
            P("dp", "tensor"),
            P(("dp", "tensor")),
        ),
        check_vma=False,
    )
```

profile of v0, /device:TPU:0, one launch (start us, length us, event | category | flops | bytes accessed | tf_op | source)
XLA Modules:
  0.0 955.9 jit_solution(9160846206304437627)
XLA Ops:
  17.8 38.8 %all-reduce.17 = (bf16[768]{0:T(1024)(128)(2,1)S(1)}, bf16[768]{0:T(1024)(128)(2,1)S(1)}, bf16[768]{0:T(1024)(128)(2,1)S(1)}, bf16[768]{0:T(1024)(128)(2,1)S(1)}...) all-reduce(bf16[768]{0:T(1024)(128)(2,1)S(1)} %dynamic-update-slice., ...), channel_id=1, replica_groups=mesh['dp'=8,'tensor'=4] {'dp'}, use_global_device_ids=true, to_apply=%add.1 | all-reduce | flops 4608 | bytes 18432
  56.6 2.1 add_convert_fusion.2
  58.8 16.6 %all-gather.1 = bf16[8,8,3]{1,2,0:T(4,128)(2,1)S(1)} all-gather(bf16[1,8,3]{1,2,0:T(4,128)(2,1)S(1)} %bitcast.145), channel_id=1, replica_groups=mesh['dp'=8,'tensor'=4] {'dp'}, dimensions={0}, use_global_device_ids=true | all-gather | bytes 432 | tf_op jit(solution)/shard_map/all_gather | solution.py:146
  75.6 17.9 %all-gather = bf16[8,8,3]{1,2,0:T(4,128)(2,1)S(1)} all-gather(bf16[1,8,3]{1,2,0:T(4,128)(2,1)S(1)} %bitcast.146), channel_id=1, replica_groups=mesh['dp'=8,'tensor'=4] {'dp'}, dimensions={0}, use_global_device_ids=true | all-gather | bytes 432 | tf_op jit(solution)/shard_map/all_gather | solution.py:149
  93.7 31.1 %all_gather.62 = bf16[768,192]{1,0:T(8,128)(2,1)S(1)} all-gather(bf16[96,192]{1,0:T(8,128)(2,1)S(1)} %copy-done.22), channel_id=1, replica_groups=mesh['dp'=8,'tensor'=4] {'dp'}, dimensions={0}, use_global_device_ids=true | all-gather | bytes 331776 | tf_op jit(solution)/shard_map/all_gather | solution.py:145
  124.8 31.1 %all_gather.64 = bf16[768,192]{1,0:T(8,128)(2,1)S(1)} all-gather(bf16[96,192]{1,0:T(8,128)(2,1)S(1)} %copy-done.23), channel_id=1, replica_groups=mesh['dp'=8,'tensor'=4] {'dp'}, dimensions={0}, use_global_device_ids=true | all-gather | bytes 331776 | tf_op jit(solution)/shard_map/all_gather | solution.py:147
  155.9 31.1 %all_gather.60 = bf16[768,192]{1,0:T(8,128)(2,1)S(1)} all-gather(bf16[96,192]{1,0:T(8,128)(2,1)S(1)} %copy-done.24), channel_id=1, replica_groups=mesh['dp'=8,'tensor'=4] {'dp'}, dimensions={0}, use_global_device_ids=true | all-gather | bytes 331776 | tf_op jit(solution)/shard_map/all_gather | solution.py:148
  187.0 31.0 %all_gather.65 = bf16[768,192]{1,0:T(8,128)(2,1)S(1)} all-gather(bf16[96,192]{1,0:T(8,128)(2,1)S(1)} %copy-done.25), channel_id=1, replica_groups=mesh['dp'=8,'tensor'=4] {'dp'}, dimensions={0}, use_global_device_ids=true | all-gather | bytes 331776 | tf_op jit(solution)/shard_map/all_gather | solution.py:150
  217.9 2.2 fusion.58
  220.2 2.2 fusion.64
  222.4 1.9 multiply_reduce_fusion.1
  224.3 2.1 exponential_reduce_fusion
  229.0 2.2 convolution_convert_fusion.3
  232.0 1.8 fusion.45
  236.3 23.1 %reduce-scatter.16.cloned.1.call-done = bf16[1,256,768]{2,1,0:T(8,128)(2,1)} async-done(((bf16[1,1024,768]{2,1,0:T(8,128)(2,1)}), bf16[1,256,768]{2,1,0:T(8,128)(2,1)}) %reduce-scatter.16.cloned.1.call-update) | async-done | bytes 393232 | tf_op jit(solution)/shard_map/reduce_scatter | solution.py:178
  261.7 1.6 add_convert_fusion.1
  264.0 2.9 fusion.106
  267.0 26.2 %all_gather.71 = bf16[64,12]{1,0:T(8,128)(2,1)S(1)} all-gather(bf16[8,12]{1,0:T(8,128)(2,1)} %param.31), channel_id=1, replica_groups=mesh['dp'=8,'tensor'=4] {'dp'}, dimensions={0}, use_global_device_ids=true | all-gather | bytes 1728 | tf_op jit(solution)/shard_map/all_gather | solution.py:155
  296.6 5.5 multiply_convert_fusion.1
  302.1 37.3 %all-gather.15.cloned.1.call-done = bf16[768,768]{1,0:T(8,128)(2,1)} async-done(((bf16[96,768]{1,0:T(8,128)(2,1)}), bf16[768,768]{1,0:T(8,128)(2,1)}) %all-gather.15.cloned.1.call-update) | async-done | bytes 1179664 | tf_op jit(solution)/shard_map/all_gather | solution.py:156
  339.4 20.3 %all-gather.17.cloned.1.call-done = bf16[1,1024,768]{2,1,0:T(8,128)(2,1)} async-done(((bf16[1,256,768]{2,1,0:T(8,128)(2,1)}), bf16[1,1024,768]{2,1,0:T(8,128)(2,1)}) %all-gather.17.cloned.1.call-update) | async-done | bytes 1572880 | tf_op jit(solution)/shard_map/all_gather | solution.py:193
  359.7 5.5 fusion.110
  366.4 2.6 fusion.47
  369.0 4.4 fusion.46
  374.7 22.6 %reduce-scatter.20.cloned.1.call-done = bf16[1,256,768]{2,1,0:T(8,128)(2,1)} async-done(((bf16[1,1024,768]{2,1,0:T(8,128)(2,1)}), bf16[1,256,768]{2,1,0:T(8,128)(2,1)}) %reduce-scatter.20.cloned.1.call-update) | async-done | bytes 393232 | tf_op jit(solution)/shard_map/reduce_scatter | solution.py:202
  397.3 2.0 fusion.89
  399.9 28.0 %reduce-scatter.18.cloned.1.call-done = bf16[1,256,768]{2,1,0:T(8,128)(2,1)} async-done(((bf16[1,1024,768]{2,1,0:T(8,128)(2,1)}), bf16[1,256,768]{2,1,0:T(8,128)(2,1)}) %reduce-scatter.18.cloned.1.call-update) | async-done | bytes 393232 | tf_op jit(solution)/shard_map/reduce_scatter | solution.py:188
  427.9 3.3 fusion.101
  433.0 19.6 %all-gather.19.cloned.1.call-done = bf16[1,1024,768]{2,1,0:T(8,128)(2,1)} async-done(((bf16[1,256,768]{2,1,0:T(8,128)(2,1)}), bf16[1,1024,768]{2,1,0:T(8,128)(2,1)}) %all-gather.19.cloned.1.call-update) | async-done | bytes 1572880 | tf_op jit(solution)/shard_map/all_gather | solution.py:211
  452.5 2.1 fusion.61
  454.6 7.5 fusion.104
  462.2 6.3 fusion.111
  468.5 19.8 %fusion.70 = bf16[3,64,1024]{2,1,0:T(8,128)(2,1)} fusion(bf16[1024,3,64]{0,2,1:T(8,128)(2,1)S(1)} %bitcast.135, f32[3,1024,1024]{1,2,0:T(8,128)} %fusion.111, f32[3,1024,1024]{1,2,0:T(8,128)} %copy-done, f32[3,1024]{1,0:T(4,128)S(1)} %log_add_fusion), kind=kOutput, calls=%fused_computation.61 | convolution fusion | flops 431165440 | bytes 25964544 | tf_op jit(solution)/shard_map/while/body/eval_jaxpr/hqk,qhd->khd/dot_general | solution.py:97
  488.3 20.0 %fusion.105 = (f32[3,64]{1,0:T(4,128)}, bf16[1024,3,64]{0,2,1:T(8,128)(2,1)}) fusion(bf16[1024,3,64]{0,2,1:T(8,128)(2,1)S(1)} %bitcast.133, f32[3,1024,1024]{1,2,0:T(8,128)} %fusion.111, f32[3,1024,1024]{1,2,0:T(8,128)} %copy-done, f32[3,1024]{1,0:T(4,128)S(1)} %log_add_fusion), kind=kOutput, calls=%fused_computation.118 | convolution fusion | flops 431361856 | bytes 25965312 | tf_op jit(solution)/shard_map/while/body/eval_jaxpr/hqk,khd->qhd/dot_general | solution.py:94
  508.3 1.7 fusion.113
  510.7 1.9 fusion.48
  512.6 4.7 fusion.29
  517.4 4.8 convolution_bitcast_fusion
  522.3 3.1 copy.76
  525.7 2.9 fusion.23
  535.0 37.5 %all-reduce.16 = (f32[64,3]{0,1:T(4,128)S(1)}, f32[64,3]{0,1:T(4,128)S(1)}, f32[64,12]{0,1:T(8,128)S(1)}) all-reduce(f32[64,3]{0,1:T(4,128)} %bitcast.144, f32[64,3]{0,1:T(4,128)} %bitcast.143, f32[64,12]{0,1:T(8,128)S(1)} %bitcast.140), channel_id=9, replica_groups=mesh['dp'=8,'tensor'=4] {'dp'}, use_global_device_ids=true, to_apply=%region_21.22.clone | all-reduce | flops 1152 | bytes 9216
  576.0 37.7 %all-reduce.15 = (f32[768]{0:T(1024)S(1)}, f32[768]{0:T(1024)S(1)}, f32[768]{0:T(1024)S(1)}, f32[768]{0:T(1024)S(1)}, f32[768]{0:T(1024)S(1)}, /*index=5*/f32[768]{0:T(1024)S(1)}) all-reduce(f32[768]{0:T(1024)S(1)} %get-tuple-element.132, f32[768]{0:T(1024)S(1)} %get-tuple-element.137, ...), channel_id=6, replica_groups=mesh['dp'=8,'tensor'=4] {'dp','tensor'}, use_global_device_ids=true, to_apply=%region_16.17.clone | all-reduce | flops 4608 | bytes 36864
  617.2 2.2 fusion.83
  619.4 66.7 %reduce-scatter.34.cloned.1.call-done = f32[96,768]{1,0:T(8,128)} async-done(((f32[768,768]{1,0:T(8,128)}), f32[96,768]{1,0:T(8,128)}) %reduce-scatter.34.cloned.1.call-update) | async-done | bytes 294928
  686.1 65.4 %reduce-scatter.30.cloned.1.call-done = f32[96,192]{1,0:T(8,128)} async-done(((f32[768,192]{1,0:T(8,128)}), f32[96,192]{1,0:T(8,128)}) %reduce-scatter.30.cloned.1.call-update) | async-done | bytes 73744 | tf_op jit(solution)/shard_map/reduce_scatter | solution.py:261
  751.5 65.8 %reduce-scatter.28.cloned.1.call-done = f32[96,192]{1,0:T(8,128)} async-done(((f32[768,192]{1,0:T(8,128)}), f32[96,192]{1,0:T(8,128)}) %reduce-scatter.28.cloned.1.call-update) | async-done | bytes 73744 | tf_op jit(solution)/shard_map/reduce_scatter | solution.py:259
  817.3 65.4 %reduce-scatter.26.cloned.1.call-done = f32[96,192]{1,0:T(8,128)} async-done(((f32[768,192]{1,0:T(8,128)}), f32[96,192]{1,0:T(8,128)}) %reduce-scatter.26.cloned.1.call-update) | async-done | bytes 73744 | tf_op jit(solution)/shard_map/reduce_scatter | solution.py:258
  882.7 65.8 %reduce-scatter.24.cloned.1.call-done = f32[96,192]{1,0:T(8,128)} async-done(((f32[768,192]{1,0:T(8,128)}), f32[96,192]{1,0:T(8,128)}) %reduce-scatter.24.cloned.1.call-update) | async-done | bytes 73744 | tf_op jit(solution)/shard_map/reduce_scatter | solution.py:256
  (165 shorter events, 40.1 us)
Async XLA Ops:
  8.0 50.8 %copy-start.31 = (bf16[8,3]{0,1:T(4,128)(2,1)S(1)}, bf16[8,3]{0,1:T(4,128)(2,1)}, u32[]{:S(2)}) copy-start(bf16[8,3]{0,1:T(4,128)(2,1)} %param.22) | copy-start | bytes 148
  8.0 67.6 %copy-start.32 = (bf16[8,3]{0,1:T(4,128)(2,1)S(1)}, bf16[8,3]{0,1:T(4,128)(2,1)}, u32[]{:S(2)}) copy-start(bf16[8,3]{0,1:T(4,128)(2,1)} %param.25) | copy-start | bytes 148
  8.0 85.7 %copy-start.22 = (bf16[96,192]{1,0:T(8,128)(2,1)S(1)}, bf16[96,192]{1,0:T(8,128)(2,1)}, u32[]{:S(2)}) copy-start(bf16[96,192]{1,0:T(8,128)(2,1)} %param.21) | copy-start | bytes 110596
  8.1 116.8 %copy-start.23 = (bf16[96,192]{1,0:T(8,128)(2,1)S(1)}, bf16[96,192]{1,0:T(8,128)(2,1)}, u32[]{:S(2)}) copy-start(bf16[96,192]{1,0:T(8,128)(2,1)} %param.23) | copy-start | bytes 110596
  8.1 147.8 %copy-start.24 = (bf16[96,192]{1,0:T(8,128)(2,1)S(1)}, bf16[96,192]{1,0:T(8,128)(2,1)}, u32[]{:S(2)}) copy-start(bf16[96,192]{1,0:T(8,128)(2,1)} %param.24) | copy-start | bytes 110596
  8.1 178.9 %copy-start.25 = (bf16[96,192]{1,0:T(8,128)(2,1)S(1)}, bf16[96,192]{1,0:T(8,128)(2,1)}, u32[]{:S(2)}) copy-start(bf16[96,192]{1,0:T(8,128)(2,1)} %param.26) | copy-start | bytes 110596
  8.1 209.9 %all-gather.9.cloned.1.call-start = ((), (), s32[]{:S(2)}) async-start(), calls=%async_computation.10 | async-start | bytes 1966080 | tf_op jit(solution)/shard_map/all_gather | solution.py:162
  9.4 49.4 %copy-start.26 = (f32[256]{0:T(256)}, f32[256]{0:T(256)S(1)}, u32[]{:S(2)}) copy-start(f32[256]{0:T(256)S(1)} %broadcast_multiply_fusion.5) | copy-start | bytes 3076
  10.8 48.0 %copy-start.29 = (f32[256]{0:T(256)}, f32[256]{0:T(256)S(1)}, u32[]{:S(2)}) copy-start(f32[256]{0:T(256)S(1)} %add_rsqrt_fusion.1) | copy-start | bytes 3076
  56.6 68.2 %copy-start.20 = (f32[768]{0:T(1024)}, f32[768]{0:T(1024)S(1)}, u32[]{:S(2)}) copy-start(f32[768]{0:T(1024)S(1)} %convert_element_type.132) | copy-start | bytes 9220
  58.8 200.6 %reduce-scatter.16.cloned.1.call-start = ((), (), s32[]{:S(2)}) async-start(), calls=%async_computation.11 | async-start | bytes 1966080 | tf_op jit(solution)/shard_map/reduce_scatter | solution.py:178
  124.8 99.5 %copy-start.12 = (bf16[768,192]{1,0:T(8,128)(2,1)}, bf16[768,192]{1,0:T(8,128)(2,1)S(1)}, u32[]{:S(2)}) copy-start(bf16[768,192]{1,0:T(8,128)(2,1)S(1)} %all_gather.62) | copy-start | bytes 884740
  155.9 68.4 %copy-start.10 = (bf16[768,192]{1,0:T(8,128)(2,1)}, bf16[768,192]{1,0:T(8,128)(2,1)S(1)}, u32[]{:S(2)}) copy-start(bf16[768,192]{1,0:T(8,128)(2,1)S(1)} %all_gather.64) | copy-start | bytes 884740
  187.0 39.4 %copy-start.7 = (bf16[768,192]{1,0:T(8,128)(2,1)}, bf16[768,192]{1,0:T(8,128)(2,1)S(1)}, u32[]{:S(2)}) copy-start(bf16[768,192]{1,0:T(8,128)(2,1)S(1)} %all_gather.60) | copy-start | bytes 884740
  217.9 13.4 %copy-start.9 = (bf16[768,192]{1,0:T(8,128)(2,1)}, bf16[768,192]{1,0:T(8,128)(2,1)S(1)}, u32[]{:S(2)}) copy-start(bf16[768,192]{1,0:T(8,128)(2,1)S(1)} %all_gather.65) | copy-start | bytes 884740
  220.2 4.1 copy-start.14
  222.4 1.9 copy-start.16
  224.3 4.7 copy-start
  224.3 2.6 copy-start.1
  231.3 28.1 %copy-start.2 = (f32[1,256,768]{2,1,0:T(8,128)S(1)}, f32[1,256,768]{2,1,0:T(8,128)}, u32[]{:S(2)}) copy-start(f32[1,256,768]{2,1,0:T(8,128)} %param.17) | copy-start | bytes 2359300
  233.9 62.7 %all-gather.13.cloned.1.call-start = ((), (), s32[]{:S(2)}) async-start(), calls=%async_computation.13 | async-start | bytes 1327104 | tf_op jit(solution)/shard_map/all_gather | solution.py:154
  234.5 62.1 %all-gather.11.cloned.1.call-start = ((), (), s32[]{:S(2)}) async-start(), calls=%async_computation.12 | async-start | bytes 1966080 | tf_op jit(solution)/shard_map/all_gather | solution.py:183
  263.4 76.0 %all-gather.15.cloned.1.call-start = ((), (), s32[]{:S(2)}) async-start(), calls=%async_computation.14 | async-start | bytes 1327104 | tf_op jit(solution)/shard_map/all_gather | solution.py:156
  264.0 95.7 %all-gather.17.cloned.1.call-start = ((), (), s32[]{:S(2)}) async-start(), calls=%async_computation.16 | async-start | bytes 1966080 | tf_op jit(solution)/shard_map/all_gather | solution.py:193
  266.9 130.4 %reduce-scatter.20.cloned.1.call-start = ((), (), s32[]{:S(2)}) async-start(), calls=%async_computation.17 | async-start | bytes 1966080 | tf_op jit(solution)/shard_map/reduce_scatter | solution.py:202
  359.7 6.7 copy-start.33
  365.2 1.2 copy-start.34
  369.0 59.0 %reduce-scatter.18.cloned.1.call-start = ((), (), s32[]{:S(2)}) async-start(), calls=%async_computation.15 | async-start | bytes 1966080 | tf_op jit(solution)/shard_map/reduce_scatter | solution.py:188
  373.4 79.1 %all-gather.19.cloned.1.call-start = ((), (), s32[]{:S(2)}) async-start(), calls=%async_computation.18 | async-start | bytes 1966080 | tf_op jit(solution)/shard_map/all_gather | solution.py:211
  431.2 0.9 copy-start.3
  432.9 141.7 %reduce-scatter.22.cloned.1.call-start = ((), (), s32[]{:S(2)}) async-start(), calls=%async_computation.19 | async-start | bytes 1966080 | tf_op jit(solution)/shard_map/reduce_scatter | solution.py:236
  462.2 6.3 copy-start.17
  468.5 19.8 %copy-start.15 = (bf16[1024,192]{0,1:T(8,128)(2,1)S(1)}, bf16[1024,192]{0,1:T(8,128)(2,1)}, u32[]{:S(2)}) copy-start(bf16[1024,192]{0,1:T(8,128)(2,1)} %copy-done.14) | copy-start | bytes 1179652
  488.3 20.0 %copy-start.11 = (bf16[768,192]{1,0:T(8,128)(2,1)S(1)}, bf16[768,192]{1,0:T(8,128)(2,1)}, u32[]{:S(2)}) copy-start(bf16[768,192]{1,0:T(8,128)(2,1)} %copy-done.10) | copy-start | bytes 884740
  508.3 1.7 copy-start.13
  508.3 1.7 copy-start.18
  508.3 2.4 copy-start.8
  512.6 106.8 %reduce-scatter.32.cloned.1.call-start = ((), (), s32[]{:S(2)}) async-start(), calls=%async_computation.24 | async-start | bytes 2654208 | tf_op jit(solution)/shard_map/reduce_scatter | solution.py:262
  517.4 168.7 %reduce-scatter.34.cloned.1.call-start = ((), (), s32[]{:S(2)}) async-start(), calls=%async_computation.25 | async-start | bytes 2654208
  522.3 3.4 copy-start.6
  525.4 226.1 %reduce-scatter.30.cloned.1.call-start = ((), (), s32[]{:S(2)}) async-start(), calls=%async_computation.23 | async-start | bytes 884736 | tf_op jit(solution)/shard_map/reduce_scatter | solution.py:261
  528.6 1.7 copy-start.19
  528.6 288.7 %reduce-scatter.28.cloned.1.call-start = ((), (), s32[]{:S(2)}) async-start(), calls=%async_computation.22 | async-start | bytes 884736 | tf_op jit(solution)/shard_map/reduce_scatter | solution.py:259
  530.2 44.3 %copy-start.21 = (f32[768]{0:T(1024)S(1)}, f32[768]{0:T(1024)}, u32[]{:S(2)}) copy-start(f32[768]{0:T(1024)} %copy-done.20) | copy-start | bytes 9220
  530.2 44.3 %copy-start.27 = (f32[256]{0:T(256)S(1)}, f32[256]{0:T(256)}, u32[]{:S(2)}) copy-start(f32[256]{0:T(256)} %copy-done.26) | copy-start | bytes 3076
  530.3 352.4 %reduce-scatter.26.cloned.1.call-start = ((), (), s32[]{:S(2)}) async-start(), calls=%async_computation.21 | async-start | bytes 884736 | tf_op jit(solution)/shard_map/reduce_scatter | solution.py:258
  531.9 85.3 %copy-start.4 = (f32[1,256,768]{2,1,0:T(8,128)S(1)}, f32[1,256,768]{2,1,0:T(8,128)}, u32[]{:S(2)}) copy-start(f32[1,256,768]{2,1,0:T(8,128)} %copy-done.3) | copy-start | bytes 2359300
  531.9 416.6 %reduce-scatter.24.cloned.1.call-start = ((), (), s32[]{:S(2)}) async-start(), calls=%async_computation.20 | async-start | bytes 884736 | tf_op jit(solution)/shard_map/reduce_scatter | solution.py:256
  (3 other events, 1.9 us)
Sparse Core Ops, SparseCore 0:
  58.9 16.9 all-gather.8
  234.0 25.3 reduce-scatter.15
  369.1 28.1 reduce-scatter.19
  399.7 28.1 reduce-scatter.17
Sparse Core Ops, SparseCore 1:
  236.8 38.6 all-gather.12
  277.6 18.0 all-gather.10
  297.9 41.5 all-gather.14
  341.7 18.0 all-gather.16
  433.0 19.5 all-gather.18
  512.7 28.1 reduce-scatter.21
  544.7 69.3 reduce-scatter.31
  618.0 68.0 reduce-scatter.33
  689.9 61.6 reduce-scatter.29
  755.8 61.5 reduce-scatter.27
  821.1 61.5 reduce-scatter.25
  886.9 61.5 reduce-scatter.23
where the time goes:
time: 965 us; the launch traced here: 956 us
  waiting for transfers between devices  481 us (50%)
  blocking collectives  299 us (31%)
  matrix products  106 us (11%)
  other arithmetic  26.7 us (3%)
  local copies, waits for them, and re-layouts  24.5 us (3%)
  between operations  17.4 us (2%)
    unnamed x3, blocking collectives  114 us
    unnamed x17, waiting for transfers between devices  67.5 us
    reduce_scatter x1, waiting for transfers between devices, on_device(): lax.psum_scatter(query_grad_part, 'dp', scatter_dimension=0, tiled=True)  65.8 us
    reduce_scatter x1, waiting for transfers between devices, on_device(): lax.psum_scatter(value_grad_part, 'dp', scatter_dimension=0, tiled=True)  65.8 us
    reduce_scatter x1, waiting for transfers between devices, on_device(): lax.psum_scatter(output_grad, 'dp', scatter_dimension=0, tiled=True)  65.4 us
    reduce_scatter x1, waiting for transfers between devices, on_device(): lax.psum_scatter(key_grad_part, 'dp', scatter_dimension=0, tiled=True)  65.4 us
    all_gather x1, waiting for transfers between devices, on_device(): lax.all_gather(outer_weight, 'dp', axis=0, tiled=True)  37.3 us
    dot_general x12, matrix products, matmul(): return jnp.dot(left, right, preferred_element_type=jnp.float32)  31.2 us
  transfers between devices with their start and end apart: 16, of which 11 were waited for; matrix products, arithmetic and copies ran while one was open for 6% of the time, Pallas kernels for 0%

commit v1 on v0

--- a/solution.py
+++ b/solution.py
@@ -8,6 +8,28 @@
 EPS = 1e-05
 ROOT_HALF = 0.7071067811865476
 DENSITY_NORM = 0.3989422804014327
+
+
+def joined_along(parts, dim):
+    shape = list(parts.shape[1:])
+    shape[dim] *= parts.shape[0]
+    return jnp.moveaxis(parts, 0, dim).reshape(shape)
+
+
+def grow_blocks(array, axis):
+    peers = lax.axis_size(axis)
+    parts = array[None]
+    for level in range(peers.bit_length() - 1):
+        apart = 1 << level
+        other = lax.ppermute(parts, axis, [(i, i ^ apart) for i in range(peers)])
+        both = jnp.stack([parts, other])
+        upper = lax.axis_index(axis) >> level & 1
+        parts = jnp.where(upper == 0, both, both[::-1]).reshape(-1, *array.shape)
+    return parts
+
+
+def gather_by_bits(shard, axis, dim):
+    return joined_along(grow_blocks(shard, axis), dim)
 
 
 def layer_norm(block, gain, shift):
@@ -153,7 +175,7 @@
         lax.all_gather(feed_shift, "dp", axis=0, tiled=True),
         lax.all_gather(inner_weight, "dp", axis=0, tiled=True),
         lax.all_gather(inner_bias, "dp", axis=0, tiled=True),
-        lax.all_gather(outer_weight, "dp", axis=0, tiled=True),
+        gather_by_bits(outer_weight, "dp", 0),
         lax.all_gather(outer_bias, "dp", axis=0, tiled=True),
     )
     clip_count = layer_input.shape[0]

time: 965 us -> 947 us (0.981)
  waiting for transfers between devices: 481 us -> 432 us
  blocking collectives: 299 us -> 317 us
    all_gather x1 -> x0, waiting for transfers between devices: 37.3 us -> none  [on_device(): lax.all_gather(outer_weight, 'dp', axis=0, tiled=True)]
    all_gather x1, waiting for transfers between devices: 20.3 us -> 0.01 us  [on_device(): lax.all_gather(cot_low, 'tensor', axis=1, tiled=True)]
    all_gather x1, blocking collectives: 26.2 us -> 43.3 us  [on_device(): lax.all_gather(inner_bias, 'dp', axis=0, tiled=True)]
    ppermute x0 -> x3, waiting for transfers between devices: none -> 9.85 us  [grow_blocks(): other = lax.ppermute(parts, axis, [(i, i ^ apart) for i in range(peers)])]
    unnamed x17 -> x16, waiting for transfers between devices: 67.5 us -> 67.9 us
  transfers between devices with their start and end apart: 16 -> 18, of which waited for: 11 -> 11; matrix products, arithmetic and copies ran while one was open for 6% -> 7% of each run, Pallas kernels for 0% -> 0%
where the time goes in v1:
time: 947 us; the launch traced here: 937 us
  waiting for transfers between devices  432 us (46%)
  blocking collectives  317 us (33%)
  matrix products  106 us (11%)
  other arithmetic  33.3 us (4%)
  local copies, waits for them, and re-layouts  24.6 us (3%)
  between operations  17.6 us (2%)
    unnamed x3, blocking collectives  115 us
    unnamed x16, waiting for transfers between devices  67.9 us
    reduce_scatter x1, waiting for transfers between devices, on_device(): lax.psum_scatter(value_grad_part, 'dp', scatter_dimension=0, tiled=True)  65.7 us
    reduce_scatter x1, waiting for transfers between devices, on_device(): lax.psum_scatter(query_grad_part, 'dp', scatter_dimension=0, tiled=True)  65.7 us
    reduce_scatter x1, waiting for transfers between devices, on_device(): lax.psum_scatter(key_grad_part, 'dp', scatter_dimension=0, tiled=True)  65.5 us
    reduce_scatter x1, waiting for transfers between devices, on_device(): lax.psum_scatter(output_grad, 'dp', scatter_dimension=0, tiled=True)  65.4 us
    all_gather x1, blocking collectives, on_device(): lax.all_gather(inner_bias, 'dp', axis=0, tiled=True)  43.3 us
    dot_general x12, matrix products, matmul(): return jnp.dot(left, right, preferred_element_type=jnp.float32)  31.2 us
  transfers between devices with their start and end apart: 18, of which 11 were waited for; matrix products, arithmetic and copies ran while one was open for 7% of the time, Pallas kernels for 0%

profile of v1, /device:TPU:0, one launch (start us, length us, event | category | flops | bytes accessed | tf_op | source)
XLA Modules:
  0.0 937.0 jit_solution(1337025346662386990)
XLA Ops:
  17.8 38.8 %all-reduce.17 = (bf16[768]{0:T(1024)(128)(2,1)S(1)}, bf16[768]{0:T(1024)(128)(2,1)S(1)}, bf16[768]{0:T(1024)(128)(2,1)S(1)}, bf16[768]{0:T(1024)(128)(2,1)S(1)}...) all-reduce(bf16[768]{0:T(1024)(128)(2,1)S(1)} %dynamic-update-slice., ...), channel_id=1, replica_groups=mesh['dp'=8,'tensor'=4] {'dp'}, use_global_device_ids=true, to_apply=%add.1 | all-reduce | flops 4608 | bytes 18432
  56.6 2.1 add_convert_fusion.2
  58.8 16.6 %all-gather.1 = bf16[8,8,3]{1,2,0:T(4,128)(2,1)S(1)} all-gather(bf16[1,8,3]{1,2,0:T(4,128)(2,1)S(1)} %bitcast.163), channel_id=1, replica_groups=mesh['dp'=8,'tensor'=4] {'dp'}, dimensions={0}, use_global_device_ids=true | all-gather | bytes 432 | tf_op jit(solution)/shard_map/all_gather | solution.py:168
  75.6 17.9 %all-gather = bf16[8,8,3]{1,2,0:T(4,128)(2,1)S(1)} all-gather(bf16[1,8,3]{1,2,0:T(4,128)(2,1)S(1)} %bitcast.164), channel_id=1, replica_groups=mesh['dp'=8,'tensor'=4] {'dp'}, dimensions={0}, use_global_device_ids=true | all-gather | bytes 432 | tf_op jit(solution)/shard_map/all_gather | solution.py:171
  93.7 31.1 %all_gather.59 = bf16[768,192]{1,0:T(8,128)(2,1)S(1)} all-gather(bf16[96,192]{1,0:T(8,128)(2,1)S(1)} %copy-done.22), channel_id=1, replica_groups=mesh['dp'=8,'tensor'=4] {'dp'}, dimensions={0}, use_global_device_ids=true | all-gather | bytes 331776 | tf_op jit(solution)/shard_map/all_gather | solution.py:167
  124.8 31.1 %all_gather.61 = bf16[768,192]{1,0:T(8,128)(2,1)S(1)} all-gather(bf16[96,192]{1,0:T(8,128)(2,1)S(1)} %copy-done.23), channel_id=1, replica_groups=mesh['dp'=8,'tensor'=4] {'dp'}, dimensions={0}, use_global_device_ids=true | all-gather | bytes 331776 | tf_op jit(solution)/shard_map/all_gather | solution.py:169
  155.9 31.1 %all_gather.57 = bf16[768,192]{1,0:T(8,128)(2,1)S(1)} all-gather(bf16[96,192]{1,0:T(8,128)(2,1)S(1)} %copy-done.24), channel_id=1, replica_groups=mesh['dp'=8,'tensor'=4] {'dp'}, dimensions={0}, use_global_device_ids=true | all-gather | bytes 331776 | tf_op jit(solution)/shard_map/all_gather | solution.py:170
  187.0 31.0 %all_gather.62 = bf16[768,192]{1,0:T(8,128)(2,1)S(1)} all-gather(bf16[96,192]{1,0:T(8,128)(2,1)S(1)} %copy-done.25), channel_id=1, replica_groups=mesh['dp'=8,'tensor'=4] {'dp'}, dimensions={0}, use_global_device_ids=true | all-gather | bytes 331776 | tf_op jit(solution)/shard_map/all_gather | solution.py:172
  217.9 2.2 fusion.58
  220.2 2.2 fusion.64
  222.4 1.9 multiply_reduce_fusion.1
  224.3 2.1 exponential_reduce_fusion
  229.0 2.2 convolution_convert_fusion.3
  232.0 1.8 fusion.45
  236.3 23.1 %reduce-scatter.16.cloned.1.call-done = bf16[1,256,768]{2,1,0:T(8,128)(2,1)} async-done(((bf16[1,1024,768]{2,1,0:T(8,128)(2,1)}), bf16[1,256,768]{2,1,0:T(8,128)(2,1)}) %reduce-scatter.16.cloned.1.call-update) | async-done | bytes 393232 | tf_op jit(solution)/shard_map/reduce_scatter | solution.py:200
  265.5 2.9 fusion.108
  268.5 2.4 collective-permute-done
  274.2 7.5 collective-permute-done.1
  283.7 2.4 collective-permute-start.2
  286.2 43.3 %all_gather.68 = bf16[64,12]{1,0:T(8,128)(2,1)S(1)} all-gather(bf16[8,12]{1,0:T(8,128)(2,1)} %param.31), channel_id=1, replica_groups=mesh['dp'=8,'tensor'=4] {'dp'}, dimensions={0}, use_global_device_ids=true | all-gather | bytes 1728 | tf_op jit(solution)/shard_map/all_gather | solution.py:177
  335.5 5.5 multiply_convert_fusion.1
  341.0 5.5 fusion.112
  347.7 2.6 fusion.47
  350.3 4.4 fusion.46
  356.0 21.2 %reduce-scatter.20.cloned.1.call-done = bf16[1,256,768]{2,1,0:T(8,128)(2,1)} async-done(((bf16[1,1024,768]{2,1,0:T(8,128)(2,1)}), bf16[1,256,768]{2,1,0:T(8,128)(2,1)}) %reduce-scatter.20.cloned.1.call-update) | async-done | bytes 393232 | tf_op jit(solution)/shard_map/reduce_scatter | solution.py:224
  377.2 2.0 fusion.89
  379.8 28.0 %reduce-scatter.18.cloned.1.call-done = bf16[1,256,768]{2,1,0:T(8,128)(2,1)} async-done(((bf16[1,1024,768]{2,1,0:T(8,128)(2,1)}), bf16[1,256,768]{2,1,0:T(8,128)(2,1)}) %reduce-scatter.18.cloned.1.call-update) | async-done | bytes 393232 | tf_op jit(solution)/shard_map/reduce_scatter | solution.py:210
  407.8 3.3 fusion.103
  412.9 19.6 %all-gather.16.cloned.1.call-done = bf16[1,1024,768]{2,1,0:T(8,128)(2,1)} async-done(((bf16[1,256,768]{2,1,0:T(8,128)(2,1)}), bf16[1,1024,768]{2,1,0:T(8,128)(2,1)}) %all-gather.16.cloned.1.call-update) | async-done | bytes 1572880 | tf_op jit(solution)/shard_map/all_gather | solution.py:233
  432.4 2.1 fusion.61
  434.6 7.5 fusion.106
  442.1 6.3 fusion.113
  448.4 19.8 %fusion.70 = bf16[3,64,1024]{2,1,0:T(8,128)(2,1)} fusion(bf16[1024,3,64]{0,2,1:T(8,128)(2,1)S(1)} %bitcast.149, f32[3,1024,1024]{1,2,0:T(8,128)} %fusion.113, f32[3,1024,1024]{1,2,0:T(8,128)} %copy-done, f32[3,1024]{1,0:T(4,128)S(1)} %log_add_fusion), kind=kOutput, calls=%fused_computation.62 | convolution fusion | flops 431165440 | bytes 25964544 | tf_op jit(solution)/shard_map/while/body/eval_jaxpr/hqk,qhd->khd/dot_general | solution.py:119
  468.2 20.0 %fusion.107 = (f32[3,64]{1,0:T(4,128)}, bf16[1024,3,64]{0,2,1:T(8,128)(2,1)}) fusion(bf16[1024,3,64]{0,2,1:T(8,128)(2,1)S(1)} %bitcast.147, f32[3,1024,1024]{1,2,0:T(8,128)} %fusion.113, f32[3,1024,1024]{1,2,0:T(8,128)} %copy-done, f32[3,1024]{1,0:T(4,128)S(1)} %log_add_fusion), kind=kOutput, calls=%fused_computation.126 | convolution fusion | flops 431361856 | bytes 25965312 | tf_op jit(solution)/shard_map/while/body/eval_jaxpr/hqk,khd->qhd/dot_general | solution.py:116
  488.3 1.7 fusion.115
  490.6 1.9 fusion.48
  492.6 4.7 fusion.29
  497.4 4.8 convolution_bitcast_fusion
  502.2 3.1 copy.81
  505.6 2.9 fusion.23
  514.9 37.6 %all-reduce.16 = (f32[64,3]{0,1:T(4,128)S(1)}, f32[64,3]{0,1:T(4,128)S(1)}, f32[64,12]{0,1:T(8,128)S(1)}) all-reduce(f32[64,3]{0,1:T(4,128)} %bitcast.162, f32[64,3]{0,1:T(4,128)} %bitcast.161, f32[64,12]{0,1:T(8,128)S(1)} %bitcast.158), channel_id=9, replica_groups=mesh['dp'=8,'tensor'=4] {'dp'}, use_global_device_ids=true, to_apply=%region_21.22.clone | all-reduce | flops 1152 | bytes 9216
  556.0 38.3 %all-reduce.15 = (f32[768]{0:T(1024)S(1)}, f32[768]{0:T(1024)S(1)}, f32[768]{0:T(1024)S(1)}, f32[768]{0:T(1024)S(1)}, f32[768]{0:T(1024)S(1)}, /*index=5*/f32[768]{0:T(1024)S(1)}) all-reduce(f32[768]{0:T(1024)S(1)} %get-tuple-element.132, f32[768]{0:T(1024)S(1)} %get-tuple-element.137, ...), channel_id=6, replica_groups=mesh['dp'=8,'tensor'=4] {'dp','tensor'}, use_global_device_ids=true, to_apply=%region_16.17.clone | all-reduce | flops 4608 | bytes 36864
  597.8 2.2 fusion.83
  600.0 67.2 %reduce-scatter.34.cloned.1.call-done = f32[96,768]{1,0:T(8,128)} async-done(((f32[768,768]{1,0:T(8,128)}), f32[96,768]{1,0:T(8,128)}) %reduce-scatter.34.cloned.1.call-update) | async-done | bytes 294928
  667.1 65.4 %reduce-scatter.30.cloned.1.call-done = f32[96,192]{1,0:T(8,128)} async-done(((f32[768,192]{1,0:T(8,128)}), f32[96,192]{1,0:T(8,128)}) %reduce-scatter.30.cloned.1.call-update) | async-done | bytes 73744 | tf_op jit(solution)/shard_map/reduce_scatter | solution.py:283
  732.5 65.7 %reduce-scatter.28.cloned.1.call-done = f32[96,192]{1,0:T(8,128)} async-done(((f32[768,192]{1,0:T(8,128)}), f32[96,192]{1,0:T(8,128)}) %reduce-scatter.28.cloned.1.call-update) | async-done | bytes 73744 | tf_op jit(solution)/shard_map/reduce_scatter | solution.py:281
  798.3 65.5 %reduce-scatter.26.cloned.1.call-done = f32[96,192]{1,0:T(8,128)} async-done(((f32[768,192]{1,0:T(8,128)}), f32[96,192]{1,0:T(8,128)}) %reduce-scatter.26.cloned.1.call-update) | async-done | bytes 73744 | tf_op jit(solution)/shard_map/reduce_scatter | solution.py:280
  863.8 65.7 %reduce-scatter.24.cloned.1.call-done = f32[96,192]{1,0:T(8,128)} async-done(((f32[768,192]{1,0:T(8,128)}), f32[96,192]{1,0:T(8,128)}) %reduce-scatter.24.cloned.1.call-update) | async-done | bytes 73744 | tf_op jit(solution)/shard_map/reduce_scatter | solution.py:278
  (174 shorter events, 51.2 us)
Async XLA Ops:
  8.0 50.8 %copy-start.31 = (bf16[8,3]{0,1:T(4,128)(2,1)S(1)}, bf16[8,3]{0,1:T(4,128)(2,1)}, u32[]{:S(2)}) copy-start(bf16[8,3]{0,1:T(4,128)(2,1)} %param.22) | copy-start | bytes 148
  8.0 67.6 %copy-start.32 = (bf16[8,3]{0,1:T(4,128)(2,1)S(1)}, bf16[8,3]{0,1:T(4,128)(2,1)}, u32[]{:S(2)}) copy-start(bf16[8,3]{0,1:T(4,128)(2,1)} %param.25) | copy-start | bytes 148
  8.0 85.7 %copy-start.22 = (bf16[96,192]{1,0:T(8,128)(2,1)S(1)}, bf16[96,192]{1,0:T(8,128)(2,1)}, u32[]{:S(2)}) copy-start(bf16[96,192]{1,0:T(8,128)(2,1)} %param.21) | copy-start | bytes 110596
  8.1 116.8 %copy-start.23 = (bf16[96,192]{1,0:T(8,128)(2,1)S(1)}, bf16[96,192]{1,0:T(8,128)(2,1)}, u32[]{:S(2)}) copy-start(bf16[96,192]{1,0:T(8,128)(2,1)} %param.23) | copy-start | bytes 110596
  8.1 147.8 %copy-start.24 = (bf16[96,192]{1,0:T(8,128)(2,1)S(1)}, bf16[96,192]{1,0:T(8,128)(2,1)}, u32[]{:S(2)}) copy-start(bf16[96,192]{1,0:T(8,128)(2,1)} %param.24) | copy-start | bytes 110596
  8.1 178.9 %copy-start.25 = (bf16[96,192]{1,0:T(8,128)(2,1)S(1)}, bf16[96,192]{1,0:T(8,128)(2,1)}, u32[]{:S(2)}) copy-start(bf16[96,192]{1,0:T(8,128)(2,1)} %param.26) | copy-start | bytes 110596
  8.1 209.9 %all-gather.8.cloned.1.call-start = ((), (), s32[]{:S(2)}) async-start(), calls=%async_computation.10 | async-start | bytes 1966080 | tf_op jit(solution)/shard_map/all_gather | solution.py:184
  9.4 49.4 %copy-start.26 = (f32[256]{0:T(256)}, f32[256]{0:T(256)S(1)}, u32[]{:S(2)}) copy-start(f32[256]{0:T(256)S(1)} %broadcast_multiply_fusion.5) | copy-start | bytes 3076
  10.8 48.0 %copy-start.29 = (f32[256]{0:T(256)}, f32[256]{0:T(256)S(1)}, u32[]{:S(2)}) copy-start(f32[256]{0:T(256)S(1)} %add_rsqrt_fusion.1) | copy-start | bytes 3076
  56.6 68.2 %copy-start.20 = (f32[768]{0:T(1024)}, f32[768]{0:T(1024)S(1)}, u32[]{:S(2)}) copy-start(f32[768]{0:T(1024)S(1)} %convert_element_type.132) | copy-start | bytes 9220
  58.8 200.6 %reduce-scatter.16.cloned.1.call-start = ((), (), s32[]{:S(2)}) async-start(), calls=%async_computation.11 | async-start | bytes 1966080 | tf_op jit(solution)/shard_map/reduce_scatter | solution.py:200
  124.8 99.5 %copy-start.12 = (bf16[768,192]{1,0:T(8,128)(2,1)}, bf16[768,192]{1,0:T(8,128)(2,1)S(1)}, u32[]{:S(2)}) copy-start(bf16[768,192]{1,0:T(8,128)(2,1)S(1)} %all_gather.59) | copy-start | bytes 884740
  155.9 68.4 %copy-start.10 = (bf16[768,192]{1,0:T(8,128)(2,1)}, bf16[768,192]{1,0:T(8,128)(2,1)S(1)}, u32[]{:S(2)}) copy-start(bf16[768,192]{1,0:T(8,128)(2,1)S(1)} %all_gather.61) | copy-start | bytes 884740
  187.0 39.4 %copy-start.7 = (bf16[768,192]{1,0:T(8,128)(2,1)}, bf16[768,192]{1,0:T(8,128)(2,1)S(1)}, u32[]{:S(2)}) copy-start(bf16[768,192]{1,0:T(8,128)(2,1)S(1)} %all_gather.57) | copy-start | bytes 884740
  217.9 13.4 %copy-start.9 = (bf16[768,192]{1,0:T(8,128)(2,1)}, bf16[768,192]{1,0:T(8,128)(2,1)S(1)}, u32[]{:S(2)}) copy-start(bf16[768,192]{1,0:T(8,128)(2,1)S(1)} %all_gather.62) | copy-start | bytes 884740
  220.2 4.1 copy-start.14
  222.4 1.9 copy-start.16
  224.3 4.7 copy-start
  224.3 2.6 copy-start.1
  231.3 28.1 %copy-start.2 = (f32[1,256,768]{2,1,0:T(8,128)S(1)}, f32[1,256,768]{2,1,0:T(8,128)}, u32[]{:S(2)}) copy-start(f32[1,256,768]{2,1,0:T(8,128)} %param.17) | copy-start | bytes 2359300
  233.9 101.6 %all-gather.12.cloned.1.call-start = ((), (), s32[]{:S(2)}) async-start(), calls=%async_computation.13 | async-start | bytes 1327104 | tf_op jit(solution)/shard_map/all_gather | solution.py:176
  234.5 101.0 %all-gather.10.cloned.1.call-start = ((), (), s32[]{:S(2)}) async-start(), calls=%async_computation.12 | async-start | bytes 1966080 | tf_op jit(solution)/shard_map/all_gather | solution.py:205
  263.4 77.6 %all-gather.14.cloned.1.call-start = ((), (), s32[]{:S(2)}) async-start(), calls=%async_computation.15 | async-start | bytes 1966080 | tf_op jit(solution)/shard_map/all_gather | solution.py:215
  263.9 6.9 collective-permute-start
  268.4 108.8 %reduce-scatter.20.cloned.1.call-start = ((), (), s32[]{:S(2)}) async-start(), calls=%async_computation.16 | async-start | bytes 1966080 | tf_op jit(solution)/shard_map/reduce_scatter | solution.py:224
  272.7 8.9 collective-permute-start.1
  283.7 49.2 %collective-permute-start.2 = (bf16[4,96,768]{2,1,0:T(8,128)(2,1)}, bf16[4,96,768]{2,1,0:T(8,128)(2,1)}, u32[]{:S(2)}, u32[]{:S(2)}) collective-permute-start(bf16[4,96,768]{2,1,0:T(8,128)(2,1)} %bitcast.21), channel_id=1, source_target_pairs={{0,16},{4,20},{8,24},{12,28},{16,0},{20,4},{24,8},{28,12},{1,17},{... | collective-permute-start | bytes 1769480 | tf_op jit(solution)/shard_map/ppermute | solution.py:24
  341.0 6.7 copy-start.33
  350.3 57.6 %reduce-scatter.18.cloned.1.call-start = ((), (), s32[]{:S(2)}) async-start(), calls=%async_computation.14 | async-start | bytes 1966080 | tf_op jit(solution)/shard_map/reduce_scatter | solution.py:210
  354.7 77.8 %all-gather.16.cloned.1.call-start = ((), (), s32[]{:S(2)}) async-start(), calls=%async_computation.17 | async-start | bytes 1966080 | tf_op jit(solution)/shard_map/all_gather | solution.py:233
  412.8 141.7 %reduce-scatter.22.cloned.1.call-start = ((), (), s32[]{:S(2)}) async-start(), calls=%async_computation.18 | async-start | bytes 1966080 | tf_op jit(solution)/shard_map/reduce_scatter | solution.py:258
  442.1 6.3 copy-start.17
  448.4 19.8 %copy-start.15 = (bf16[1024,192]{0,1:T(8,128)(2,1)S(1)}, bf16[1024,192]{0,1:T(8,128)(2,1)}, u32[]{:S(2)}) copy-start(bf16[1024,192]{0,1:T(8,128)(2,1)} %copy-done.14) | copy-start | bytes 1179652
  468.2 20.0 %copy-start.11 = (bf16[768,192]{1,0:T(8,128)(2,1)S(1)}, bf16[768,192]{1,0:T(8,128)(2,1)}, u32[]{:S(2)}) copy-start(bf16[768,192]{1,0:T(8,128)(2,1)} %copy-done.10) | copy-start | bytes 884740
  488.2 1.7 copy-start.13
  488.2 1.7 copy-start.18
  488.2 2.4 copy-start.8
  492.5 107.5 %reduce-scatter.32.cloned.1.call-start = ((), (), s32[]{:S(2)}) async-start(), calls=%async_computation.23 | async-start | bytes 2654208 | tf_op jit(solution)/shard_map/reduce_scatter | solution.py:284
  497.3 169.8 %reduce-scatter.34.cloned.1.call-start = ((), (), s32[]{:S(2)}) async-start(), calls=%async_computation.24 | async-start | bytes 2654208
  502.2 3.4 copy-start.6
  505.3 227.2 %reduce-scatter.30.cloned.1.call-start = ((), (), s32[]{:S(2)}) async-start(), calls=%async_computation.22 | async-start | bytes 884736 | tf_op jit(solution)/shard_map/reduce_scatter | solution.py:283
  508.5 1.7 copy-start.19
  508.6 289.7 %reduce-scatter.28.cloned.1.call-start = ((), (), s32[]{:S(2)}) async-start(), calls=%async_computation.21 | async-start | bytes 884736 | tf_op jit(solution)/shard_map/reduce_scatter | solution.py:281
  510.2 44.4 %copy-start.21 = (f32[768]{0:T(1024)S(1)}, f32[768]{0:T(1024)}, u32[]{:S(2)}) copy-start(f32[768]{0:T(1024)} %copy-done.20) | copy-start | bytes 9220
  510.2 44.3 %copy-start.27 = (f32[256]{0:T(256)S(1)}, f32[256]{0:T(256)}, u32[]{:S(2)}) copy-start(f32[256]{0:T(256)} %copy-done.26) | copy-start | bytes 3076
  510.2 353.6 %reduce-scatter.26.cloned.1.call-start = ((), (), s32[]{:S(2)}) async-start(), calls=%async_computation.20 | async-start | bytes 884736 | tf_op jit(solution)/shard_map/reduce_scatter | solution.py:280
  511.8 86.0 %copy-start.4 = (f32[1,256,768]{2,1,0:T(8,128)S(1)}, f32[1,256,768]{2,1,0:T(8,128)}, u32[]{:S(2)}) copy-start(f32[1,256,768]{2,1,0:T(8,128)} %copy-done.3) | copy-start | bytes 2359300
  511.9 417.6 %reduce-scatter.24.cloned.1.call-start = ((), (), s32[]{:S(2)}) async-start(), calls=%async_computation.19 | async-start | bytes 884736 | tf_op jit(solution)/shard_map/reduce_scatter | solution.py:278
  (5 other events, 3.9 us)
Sparse Core Ops, SparseCore 0:
  58.9 16.9 all-gather.7
  234.0 25.3 reduce-scatter.15
  350.4 26.8 reduce-scatter.19
  379.6 28.1 reduce-scatter.17
Sparse Core Ops, SparseCore 1:
  236.8 38.4 all-gather.11
  277.4 18.4 all-gather.9
  297.4 19.5 all-gather.13
  412.9 19.5 all-gather.15
  492.6 28.1 reduce-scatter.21
  524.9 70.2 reduce-scatter.31
  599.0 68.1 reduce-scatter.33
  670.9 61.6 reduce-scatter.29
  736.6 61.6 reduce-scatter.27
  802.2 61.6 reduce-scatter.25
  867.9 61.5 reduce-scatter.23
